TPU v7x, 32 devices: a whole 2x2x4 slice. The times are simulated.
32 devices in a mesh: groups: 2 (over y), view: 4 (over z), gz: 2 (over x), tube: 2 (over core).
Axes of the slice: x: 2, y: 2, z: 4, core: 2. Of those that a mesh axis runs over, the one named last changes fastest.
Arguments:
- fan_views: bfloat16 [4, 2, 128, 64, 1024], P(('groups', 'tube'), 'gz', 'view'), parts along dimension 0, may hold values from -6 to 6
- offsets: int32 [4, 2, 128], P(('groups', 'tube'), 'gz', 'view'), parts along dimension 0, may hold values from 0 to 16
- rebin_matrix: bfloat16 [1024, 1024], replicated, may hold values from -0.1875 to 0.1875
- projector: bfloat16 [2, 16, 512, 256], P('tube'), as said below
- tile_index: int32 [2, 16, 2], P('tube'), may hold values from 0 to 15, as said below
- attenuation: float32 [2, 2], replicated, may hold values from 0.3 to 3
- images: float32 [2, 4, 64, 4096], P(None, ('groups', 'gz'), 'view'), parts along dimension 1, may hold values from 0.5 to 1.5
Outputs:
- sinogram: bfloat16 [4, 2, 64, 128, 1024], P(('groups', 'tube'), 'gz', 'view'), parts along dimension 0
- updated: float32 [2, 4, 64, 4096], P('tube', ('groups', 'gz'), 'view'), parts along dimension 1
There are 2 independent parts, one for each index of `groups`. A program takes and returns all parts, laid end to end along the dimension named above; an argument that names none is the same for every part. Nothing has to cross between parts.
Inputs may be any that keep to these rules, and one draw needn't show every extreme that they name: `projector`: entries are positive. `tile_index`: in each tube's list, column 0 names each of the 16 sinogram blocks once and column 1 names each of the 8 image rows 16 // 8 times.
All inputs are finite; a program needn't handle non-finite values.
Results may differ from a plain program's by a relative error of at most 0.0016.
Values may be sent and summed in bfloat16 or wider, within the bound.
A program may use at most 64 MiB of HBM per device.

v0:
```python
import jax
import jax.numpy as jnp
from jax import lax
from jax.sharding import PartitionSpec as P

DR = 64
IMG = 512
CB = 256
SUB = 4
HZ = 16
IR = 8


relax_factor = 0.8


def shifted(block, axis, distance):
    devices = range(lax.axis_size(axis))
    route = [(i - distance, i) for i in devices if i - distance in devices]
    return lax.ppermute(block, axis, route)


def rebin_rows(row_block, rebin_matrix):
    shaped = row_block.reshape(-1, row_block.shape[-1])
    rebinned = jnp.dot(shaped, rebin_matrix, preferred_element_type=jnp.float32)
    return rebinned.astype(jnp.bfloat16).reshape(row_block.shape)


def place_rows(extended, view_offsets):

    def pick_rows(view_rows, offset):
        return lax.dynamic_slice_in_dim(view_rows, HZ - offset, DR, 0)

    return jax.vmap(pick_rows, in_axes=(0, 0), out_axes=1)(extended, view_offsets)


def body(fan_views, offsets, rebin_matrix, projector, tile_index, attenuation, images):
    fan_rows = fan_views[0, 0]
    view_offsets = offsets[0, 0]
    source_rows = rebin_rows(fan_rows, rebin_matrix)
    top_rows = source_rows[:, DR - HZ :, :]
    received = shifted(top_rows, "gz", 1)
    extended = jnp.concatenate([received, source_rows], axis=1)
    placed = place_rows(extended, view_offsets)
    outgoing = placed[:, None]
    arrived = lax.all_to_all(outgoing, "view", split_axis=0, concat_axis=1, tiled=True)
    slices = arrived.shape[0]
    sinogram = arrived.reshape(slices, -1, arrived.shape[-1])
    angle_total = sinogram.shape[1]
    stride = angle_total // SUB
    measured = sinogram[:, ::stride, :].reshape(slices, -1, CB)
    block_count = measured.shape[1]
    tube_index = lax.axis_index("tube")
    weights = lax.dynamic_index_in_dim(attenuation, tube_index, 0, keepdims=False)
    material_images = images[:, 0]
    combined = (weights[0] * material_images[0] + weights[1] * material_images[1]).astype(
        jnp.bfloat16
    )
    combined = combined.reshape(slices, IR, IMG)
    tile_data = projector[0]
    index_list = tile_index[0]
    block_hot = index_list[:, 0:1] == jnp.arange(block_count, dtype=jnp.int32)[None, :]
    row_hot = index_list[:, 1:2] == jnp.arange(IR, dtype=jnp.int32)[None, :]
    chosen = jnp.einsum(
        "sqp,kq->skp", combined, row_hot.astype(jnp.bfloat16), preferred_element_type=jnp.float32
    )
    chosen = chosen.astype(jnp.bfloat16)
    projected_tiles = jnp.einsum(
        "skp,kpc->skc", chosen, tile_data, preferred_element_type=jnp.float32
    )
    projected = jnp.einsum(
        "skc,kb->sbc",
        projected_tiles,
        block_hot.astype(jnp.float32),
        precision=lax.Precision.HIGHEST,
    )
    ray_sum = jnp.einsum(
        "kc,kb->bc",
        jnp.sum(tile_data, axis=1, dtype=jnp.float32),
        block_hot.astype(jnp.float32),
        precision=lax.Precision.HIGHEST,
    )
    residual = ((measured.astype(jnp.float32) - projected) / ray_sum).astype(jnp.bfloat16)
    tile_residual = jnp.einsum(
        "sbc,kb->skc", residual, block_hot.astype(jnp.bfloat16), preferred_element_type=jnp.float32
    )
    tile_residual = tile_residual.astype(jnp.bfloat16)
    back_tiles = jnp.einsum(
        "skc,kpc->skp", tile_residual, tile_data, preferred_element_type=jnp.float32
    )
    back_projection = jnp.einsum(
        "skp,kq->sqp", back_tiles, row_hot.astype(jnp.float32), precision=lax.Precision.HIGHEST
    )
    back_projection = back_projection.reshape(slices, -1)
    pixel_sum = jnp.einsum(
        "kp,kq->qp",
        jnp.sum(tile_data, axis=2, dtype=jnp.float32),
        row_hot.astype(jnp.float32),
        precision=lax.Precision.HIGHEST,
    )
    pixel_sum = pixel_sum.reshape(-1)
    numerator = weights[:, None, None] * back_projection[None]
    denominator = weights[:, None] * pixel_sum[None]
    numerator_mine, denominator_mine = (
        lax.psum_scatter(numerator, "tube", scatter_dimension=0, tiled=True),
        lax.psum_scatter(denominator, "tube", scatter_dimension=0, tiled=True),
    )
    current = lax.dynamic_index_in_dim(material_images, tube_index, 0, keepdims=True)
    updated = current + relax_factor * (numerator_mine / denominator_mine[:, None, :])
    return (sinogram[None, None], updated[:, None])


def solution(mesh):
    in_specs = (
        P(("groups", "tube"), "gz", "view", None, None),
        P(("groups", "tube"), "gz", "view"),
        P(),
        P("tube", None, None, None),
        P("tube", None, None),
        P(),
        P(None, ("groups", "gz"), "view", None),
    )
    out_specs = (
        P(("groups", "tube"), "gz", "view", None, None),
        P("tube", ("groups", "gz"), "view", None),
    )
    return jax.shard_map(body, mesh=mesh, in_specs=in_specs, out_specs=out_specs, check_vma=False)
```

profile of v0, /device:TPU:0, one launch (start us, length us, event | category | flops | bytes accessed | tf_op | source)
XLA Modules:
  0.0 188.6 jit_solution(3790048329932212946)
XLA Ops:
  7.2 0.0 copy-start
  7.2 1.6 copy-done
  8.8 6.9 %convolution_convert_fusion = bf16[2048,1024]{1,0:T(8,128)(2,1)S(1)} fusion(bf16[2048,1024]{1,0:T(8,128)(2,1)} %bitcast.102, bf16[1024,1024]{1,0:T(8,128)(2,1)S(1)} %copy-done), kind=kOutput, calls=%fused_computation.8 | convolution fusion | flops 4297064448 | bytes 10485760 | tf_op jit(solution)/shard_map/dot_general | solution.py:25
  15.7 0.0 copy-start.4
  15.7 2.3 %copy.32 = bf16[32,64,1024]{2,0,1:T(8,128)(2,1)S(1)} copy(bf16[32,64,1024]{2,1,0:T(8,128)(2,1)S(1)} %bitcast.94) | data formatting | bytes 8388608 | tf_op jit(solution)/shard_map/reshape | solution.py:26
  18.0 0.1 slice.41
  18.1 5.1 %collective-permute-start = (bf16[32,16,1024]{2,0,1:T(8,128)(2,1)S(1)}, bf16[32,16,1024]{2,0,1:T(8,128)(2,1)S(1)}, u32[]{:S(2)}, u32[]{:S(2)}) collective-permute-start(bf16[32,16,1024]{2,0,1:T(8,128)(2,1)S(1)} %slice.41), channel_id=1, source_target_pairs={{0,2},{1,3},{4,6},{5,7},{8,10},{9,11},{12,14},{13,15},{16,18},{17,... | collective-permute-start | bytes 3145736 | tf_op jit(solution)/shard_map/ppermute | solution.py:20
  23.2 0.0 copy-done.4
  23.2 22.1 %collective-permute-done = bf16[32,16,1024]{2,0,1:T(8,128)(2,1)S(1)} collective-permute-done((bf16[32,16,1024]{2,0,1:T(8,128)(2,1)S(1)}, bf16[32,16,1024]{2,0,1:T(8,128)(2,1)S(1)}, u32[]{:S(2)}, u32[]{:S(2)}) %collective-permute-start) | collective-permute-done | bytes 1048608 | tf_op jit(solution)/shard_map/ppermute | solution.py:20
  45.4 2.7 %pad_maximum_fusion = bf16[32,80,1024]{2,0,1:T(8,128)(2,1)} fusion(bf16[32,64,1024]{2,0,1:T(8,128)(2,1)S(1)} %copy.32, bf16[32,16,1024]{2,0,1:T(8,128)(2,1)S(1)} %collective-permute-done), kind=kLoop, calls=%fused_computation.3 | loop fusion | flops 2621440 | bytes 10485760 | tf_op jit(solution)/shard_map/concatenate | solution.py:43
  48.1 12.3 %gather_fusion = bf16[32,64,1024]{2,0,1:T(8,128)(2,1)} fusion(bf16[32,80,1024]{2,0,1:T(8,128)(2,1)} %pad_maximum_fusion, s32[32]{0:T(128)S(1)} %or_bitcast_fusion), kind=kCustom, calls=%fused_computation | custom fusion | bytes 8388992 | tf_op jit(solution)/shard_map/vmap()/gather | solution.py:32
  60.4 0.0 copy-start.3
  60.4 0.0 copy-start.1
  60.4 0.0 copy-start.2
  60.4 5.0 %all-to-all-start = ((bf16[64,1,32,1024]{3,2,1,0:T(8,128)(2,1)}), bf16[64,1,32,1024]{3,2,1,0:T(8,128)(2,1)}, u32[]{:S(2)}, u32[]{:S(2)}) async-start(bf16[64,1,32,1024]{3,2,1,0:T(8,128)(2,1)} %bitcast.91), calls=%async_computation | async-start | bytes 8388608 | tf_op jit(solution)/shard_map/all_to_all | solution.py:46
  65.4 0.0 copy-start.5
  65.4 0.2 reduce-scatter.2.cloned.1.call-start
  65.7 0.0 copy-done.3
  65.7 0.6 fusion.35
  66.3 0.0 copy-done.1
  66.3 1.2 add_convert_fusion
  67.6 0.0 copy-done.2
  67.6 3.6 %convert_reduce_fusion = (f32[16,512]{1,0:T(8,128)S(1)}, f32[16,256]{1,0:T(8,128)S(1)}) fusion(bf16[1,16,512,256]{3,2,1,0:T(8,128)(2,1)} %param.10), kind=kLoop, calls=%fused_computation.1 | loop fusion | flops 6279168 | bytes 4243456 | tf_op jit(solution)/shard_map/reduce_sum | solution.py:97
  71.1 0.1 convolution_bitcast_fusion.1
  71.3 0.0 copy-done.5
  71.3 0.6 dynamic-slice.1
  71.9 0.3 fusion.21
  72.2 0.3 fusion.12
  72.4 2.9 %fusion.7 = f32[16,16,256]{2,0,1:T(8,128)S(1)} fusion(bf16[1,16,512,256]{3,2,1,0:T(8,128)(2,1)} %param.10, bf16[16,16,512]{2,1,0:T(8,128)(2,1)S(1)} %fusion.12), kind=kOutput, calls=%fused_computation.11 | convolution fusion | flops 67108864 | bytes 4718592 | tf_op jit(solution)/shard_map/skp,kpc->skc/dot_general | solution.py:68
  75.3 82.7 %all-to-all-done = bf16[64,1,32,1024]{3,2,1,0:T(8,128)(2,1)} async-done(((bf16[64,1,32,1024]{3,2,1,0:T(8,128)(2,1)}), bf16[64,1,32,1024]{3,2,1,0:T(8,128)(2,1)}, u32[]{:S(2)}, u32[]{:S(2)}) %all-to-all-start) | async-done | bytes 4194336 | tf_op jit(solution)/shard_map/all_to_all | solution.py:46
  158.0 5.0 %copy.35 = bf16[16,4,1,32,1024]{4,3,1,0,2:T(8,128)(2,1)} copy(bf16[16,4,1,32,1024]{4,3,0,1,2:T(8,128)(2,1)} %bitcast.9) | data formatting | bytes 8388608 | tf_op jit(solution)/shard_map/all_to_all | solution.py:46
  163.0 3.0 %slice.31 = bf16[16,4,1024]{2,1,0:T(4,128)(2,1)S(1)} slice(bf16[16,128,1024]{2,1,0:T(8,128)(2,1)} %bitcast.92), slice={[0:16:1], [0:128:32], [0:1024:1]} | slice | bytes 262144 | tf_op jit(solution)/shard_map/slice | solution.py:51
  166.0 0.1 reshape.74
  166.1 0.5 fusion.13
  166.5 0.2 fusion.14
  166.8 3.4 %fusion.4 = f32[16,16,512]{2,0,1:T(8,128)S(1)} fusion(bf16[1,16,512,256]{3,2,1,0:T(8,128)(2,1)} %param.10, bf16[16,16,256]{2,1,0:T(8,128)(2,1)S(1)} %fusion.14), kind=kOutput, calls=%fused_computation.9 | convolution fusion | flops 67108864 | bytes 4849664 | tf_op jit(solution)/shard_map/skc,kpc->skp/dot_general | solution.py:88
  170.2 0.6 fusion.15
  170.8 0.2 copy.45
  170.9 0.9 broadcast_multiply_fusion
  171.8 0.0 reduce-scatter.2.cloned.1.call-update
  171.9 0.1 broadcast_multiply_fusion.1
  171.9 3.4 %all-reduce.1 = f32[2,4096]{1,0:T(2,128)S(1)} all-reduce(f32[2,4096]{1,0:T(2,128)S(1)} %broadcast_multiply_fusion.1), channel_id=3, replica_groups=mesh['groups'=2,'view'=4,'gz'=2,'tube'=2] {'tube'}, use_global_device_ids=true, to_apply=%region_3.4.clone | all-reduce | flops 8192 | bytes 65536
  175.4 0.7 constant_dynamic-slice_fusion
  176.0 4.0 %reduce-scatter.2.cloned.1.call-done = f32[1,16,4096]{2,1,0:T(8,128)} async-done(((f32[2,16,4096]{2,1,0:T(8,128)}), f32[1,16,4096]{2,1,0:T(8,128)}) %reduce-scatter.2.cloned.1.call-update) | async-done | bytes 262160 | tf_op jit(solution)/shard_map/reduce_scatter | solution.py:105
  180.1 1.7 fusion.17
  (6 shorter events, 0.1 us)
Async XLA Ops:
  7.2 1.6 copy-start
  15.7 7.5 %copy-start.4 = (s32[1,1,32]{2,1,0:T(1,128)S(1)}, s32[1,1,32]{2,1,0:T(1,128)}, u32[]{:S(2)}) copy-start(s32[1,1,32]{2,1,0:T(1,128)} %param.8) | copy-start | bytes 388
  18.1 27.2 %collective-permute-start = (bf16[32,16,1024]{2,0,1:T(8,128)(2,1)S(1)}, bf16[32,16,1024]{2,0,1:T(8,128)(2,1)S(1)}, u32[]{:S(2)}, u32[]{:S(2)}) collective-permute-start(bf16[32,16,1024]{2,0,1:T(8,128)(2,1)S(1)} %slice.41), channel_id=1, source_target_pairs={{0,2},{1,3},{4,6},{5,7},{8,10},{9,11},{12,14},{13,15},{16,18},{17,... | collective-permute-start | bytes 3145736 | tf_op jit(solution)/shard_map/ppermute | solution.py:20
  60.4 5.3 %copy-start.3 = (f32[2,2]{1,0:T(2,128)S(1)}, f32[2,2]{1,0:T(2,128)}, u32[]{:S(2)}) copy-start(f32[2,2]{1,0:T(2,128)} %param.12) | copy-start | bytes 52
  60.4 5.9 %copy-start.1 = (f32[2,1,16,4096]{3,2,1,0:T(8,128)S(1)}, f32[2,1,16,4096]{3,2,1,0:T(8,128)}, u32[]{:S(2)}) copy-start(f32[2,1,16,4096]{3,2,1,0:T(8,128)} %param.13) | copy-start | bytes 1572868
  60.4 7.2 %copy-start.2 = (s32[1,16,2]{1,2,0:T(2,128)S(1)}, s32[1,16,2]{1,2,0:T(2,128)}, u32[]{:S(2)}) copy-start(s32[1,16,2]{1,2,0:T(2,128)} %param.11) | copy-start | bytes 388
  60.4 97.6 %all-to-all-start = ((bf16[64,1,32,1024]{3,2,1,0:T(8,128)(2,1)}), bf16[64,1,32,1024]{3,2,1,0:T(8,128)(2,1)}, u32[]{:S(2)}, u32[]{:S(2)}) async-start(bf16[64,1,32,1024]{3,2,1,0:T(8,128)(2,1)} %bitcast.91), calls=%async_computation | async-start | bytes 8388608 | tf_op jit(solution)/shard_map/all_to_all | solution.py:46
  65.4 5.9 %copy-start.5 = (u32[32]{0:T(128)S(1)}, u32[32]{0:T(128)}, u32[]{:S(2)}) copy-start(u32[32]{0:T(128)} %constant.56) | copy-start | bytes 388
  65.4 114.7 %reduce-scatter.2.cloned.1.call-start = ((), (), s32[]{:S(2)}) async-start(), calls=%async_computation.2 | async-start | bytes 786432 | tf_op jit(solution)/shard_map/reduce_scatter | solution.py:105
Sparse Core Ops, SparseCore 0:
  172.0 8.0 reduce-scatter.1
where the time goes:
time: 189 us
  waiting for transfers between devices  109 us (58%)
  local copies, waits for them, and re-layouts  26.4 us (14%)
  matrix products  15.1 us (8%)
  between operations  14.2 us (8%)
  starting transfers between devices  10.3 us (5%)
  other arithmetic  10.2 us (5%)
  blocking collectives  3.41 us (2%)
    all_to_all x1, waiting for transfers between devices, body(): lax.all_to_all(outgoing, 'view', split_axis=0, concat_axis=1, tiled=True)  82.7 us
    ppermute x1, waiting for transfers between devices, shifted(): return lax.ppermute(block, axis, route)  22.1 us
    gather x1, local copies, waits for them, and re-layouts, pick_rows(): return lax.dynamic_slice_in_dim(view_rows, HZ - offset, DR, 0)  12.3 us
    dot_general x1, matrix products, rebin_rows(): rebinned = jnp.dot(shaped, rebin_matrix, preferred_element_type=jnp.float32)  6.92 us
    ppermute x1, starting transfers between devices, shifted(): return lax.ppermute(block, axis, route)  5.09 us
    all_to_all x1, local copies, waits for them, and re-layouts, body(): lax.all_to_all(outgoing, 'view', split_axis=0, concat_axis=1, tiled=True)  5.01 us
    all_to_all x1, starting transfers between devices, body(): lax.all_to_all(outgoing, 'view', split_axis=0, concat_axis=1, tiled=True)  5 us
    reduce_scatter x1, waiting for transfers between devices, body(): lax.psum_scatter(numerator, 'tube', scatter_dimension=0, tiled=True)  4.05 us
  transfers between devices with their start and end apart: 3, of which 3 were waited for; matrix products, arithmetic and copies ran while one was open for 5% of the time, Pallas kernels for 0%

commit v1 on v0

v1 whole, which is shorter than its diff:
```python
import functools

import jax
import jax.numpy as jnp
from jax import lax
from jax.experimental import pallas as pl
from jax.experimental.pallas import tpu as pltpu
from jax.sharding import PartitionSpec as P

IMG = 512
CB = 256
SUB = 4
HZ = 16
IR = 8
BLK = 16
MESH = pl.DeviceIdType.MESH

relax_factor = 0.8


def kernel(
    sizes,
    offsets_ref,
    index_ref,
    weight_ref,
    fan_ref,
    rebin_ref,
    projector_ref,
    images_ref,
    sino_ref,
    updated_ref,
    ext,
    rebin,
    tiles,
    material,
    stage,
    comb,
    proj,
    picked,
    meas,
    back,
    give,
    keep,
    take,
    own_sem,
    rebin_sem,
    tiles_sem,
    image_sem,
    top_send,
    top_recv,
    out_send,
    out_recv,
    self_sem,
    picked_sem,
    tube_send,
    tube_recv,
):
    views, slabs, angles, rows, slices = sizes
    groups = angles // BLK
    blocks = rows // BLK
    share = BLK // slices
    tile_count = tiles.shape[0]
    per_angle = tile_count // SUB
    stride = views * angles // SUB
    me = lax.axis_index("view")
    slab = lax.axis_index("gz")
    tube = lax.axis_index("tube")

    def own_copy(g):
        return pltpu.make_async_copy(
            fan_ref.at[pl.ds(g * BLK, BLK)],
            ext.at[pl.ds(g * BLK, BLK), pl.ds(HZ, rows), :],
            own_sem.at[g],
        )

    rebin_copy = pltpu.make_async_copy(rebin_ref, rebin, rebin_sem)
    tiles_copy = pltpu.make_async_copy(projector_ref, tiles, tiles_sem)
    image_copy = pltpu.make_async_copy(images_ref, material, image_sem)
    own_copy(0).start()
    rebin_copy.start()
    for g in range(1, groups):
        own_copy(g).start()
    image_copy.start()
    tiles_copy.start()

    barrier = pltpu.get_barrier_semaphore()

    def greet(v, carry):
        @pl.when(v != me)
        def _():
            pl.semaphore_signal(barrier, inc=1, device_id={"view": v}, device_id_type=MESH)

        return carry

    lax.fori_loop(0, views, greet, 0)
    pl.semaphore_signal(barrier, inc=1, device_id={"tube": 1 - tube}, device_id_type=MESH)

    @pl.when(slab > 0)
    def _():
        pl.semaphore_signal(barrier, inc=1, device_id={"gz": slab - 1}, device_id_type=MESH)

    @pl.when(slab < slabs - 1)
    def _():
        pl.semaphore_signal(barrier, inc=1, device_id={"gz": slab + 1}, device_id_type=MESH)

    edges = jnp.where(slab > 0, 1, 0) + jnp.where(slab < slabs - 1, 1, 0)
    pl.semaphore_wait(barrier, views + edges)

    def top_copy(g):
        return pltpu.make_async_remote_copy(
            src_ref=fan_ref.at[pl.ds(g * BLK, BLK), pl.ds(rows - HZ, HZ), :],
            dst_ref=ext.at[pl.ds(g * BLK, BLK), pl.ds(0, HZ), :],
            send_sem=top_send.at[g],
            recv_sem=top_recv.at[g],
            device_id={"gz": jnp.minimum(slab + 1, slabs - 1)},
            device_id_type=MESH,
        )

    @pl.when(slab < slabs - 1)
    def _():
        for g in range(groups):
            top_copy(g).start()

    @pl.when(slab == 0)
    def _():
        ext[:, 0:HZ, :] = jnp.zeros((angles, HZ, ext.shape[2]), ext.dtype)

    def out_copy(g, b, j):
        return pltpu.make_async_remote_copy(
            src_ref=stage.at[g, b, pl.ds(j * slices, slices)],
            dst_ref=sino_ref.at[:, pl.ds(pl.multiple_of(me * angles + g * BLK, BLK), BLK), :],
            send_sem=out_send.at[g, b, j],
            recv_sem=out_recv.at[g, me],
            device_id={"view": b * share + j},
            device_id_type=MESH,
        )

    def self_copy(g, b, j):
        return pltpu.make_async_copy(
            stage.at[g, b, pl.ds(j * slices, slices)],
            sino_ref.at[:, pl.ds(pl.multiple_of(me * angles + g * BLK, BLK), BLK), :],
            self_sem.at[g],
        )

    def send(g, b):
        for j in range(share):
            there = b * share + j

            @pl.when(there != me)
            def _():
                out_copy(g, b, j).start()

            @pl.when(there == me)
            def _():
                self_copy(g, b, j).start()

    def sent(g, b):
        for j in range(share):

            @pl.when(b * share + j != me)
            def _():
                out_copy(g, b, j).wait_send()

    def arrived(g, v):
        @pl.when(v != me)
        def _():
            pltpu.make_async_remote_copy(
                src_ref=stage.at[g, 0, pl.ds(0, slices)],
                dst_ref=sino_ref.at[:, pl.ds(v * angles + g * BLK, BLK), :],
                send_sem=out_send.at[g, 0, 0],
                recv_sem=out_recv.at[g, v],
                device_id={"view": v},
                device_id_type=MESH,
            ).wait_recv()

        @pl.when(v == me)
        def _():
            self_copy(g, 0, 0).wait()

    half = blocks // 2
    low = me * slices // BLK < half

    def block_of(i):
        up = jnp.where(i < half, i + half, i - half + 1)
        b = jnp.where(low, up, i + 1)
        return jnp.where(i == blocks - 1, 0, b)

    def work(g):
        own_copy(g).wait()
        shape = (BLK * BLK, BLK * 2 * BLK)
        row = lax.broadcasted_iota(jnp.int32, shape, 0)
        column = lax.broadcasted_iota(jnp.int32, shape, 1)
        lane_angle = lax.broadcasted_iota(jnp.int32, (8, shape[1]), 1) >> 5
        moved = jnp.zeros((8, shape[1]), jnp.int32)
        for a in range(BLK):
            moved = jnp.where(lane_angle == a, offsets_ref[g * BLK + a], moved)
        hit = ((row & 15) == (column >> 5)) & ((row >> 4) + HZ - (column & 31) == moved[0:1])
        chosen = jnp.where(hit, 1.0, 0.0).astype(jnp.bfloat16)

        def unit(i, carry):
            b = block_of(i)

            @pl.when((i == blocks - 1) & (slab > 0))
            def _():
                top_copy(g).wait_recv()

            window = ext[pl.ds(g * BLK, BLK), pl.ds(pl.multiple_of(b * BLK, BLK), 2 * BLK), :]
            window = window.reshape(BLK * 2 * BLK, window.shape[2])
            placed = jnp.dot(chosen, window, preferred_element_type=jnp.float32)
            rebinned = jnp.dot(
                placed.astype(jnp.bfloat16), rebin[...], preferred_element_type=jnp.float32
            )
            rebinned = rebinned.astype(jnp.bfloat16)
            stage[g, b] = rebinned.reshape(BLK, BLK, rebinned.shape[1])
            if g == 0:
                send(g, b)
            return carry

        lax.fori_loop(0, blocks, unit, 0)

    rebin_copy.wait()
    for g in range(groups):
        work(g)

    image_copy.wait()
    w0 = weight_ref[tube, 0]
    w1 = weight_ref[tube, 1]
    for r in range(IR):
        part = slice(r * IMG, (r + 1) * IMG)
        mixed = (w0 * material[0, :, part] + w1 * material[1, :, part]).astype(jnp.bfloat16)
        comb[r, 0:BLK] = mixed
        comb[r, BLK : 2 * BLK] = jnp.ones((BLK, IMG), jnp.bfloat16)
    tiles_copy.wait()

    def forward(k, carry):
        proj[k] = jnp.dot(comb[index_ref[k, 1]], tiles[k], preferred_element_type=jnp.float32)
        return carry

    lax.fori_loop(0, tile_count, forward, 0)

    for g in range(1, groups):

        def follow(i, carry):
            b = block_of(i)
            sent(g - 1, b)
            send(g, b)
            return carry

        lax.fori_loop(0, blocks, follow, 0)

    early = []
    for q in range(SUB):
        v, local = divmod(q * stride, angles)
        if (local // BLK, v) not in early:
            early.append((local // BLK, v))
            arrived(local // BLK, v)
    fetches = [
        pltpu.make_async_copy(
            sino_ref.at[:, pl.ds(q * stride // BLK * BLK, BLK), :],
            picked.at[q],
            picked_sem.at[q],
        )
        for q in range(SUB)
    ]
    for fetch in fetches:
        fetch.start()
    for q in range(SUB):
        fetches[q].wait()
        shape = (BLK, slices * BLK)
        row = lax.broadcasted_iota(jnp.int32, shape, 0)
        column = lax.broadcasted_iota(jnp.int32, shape, 1)
        pick = jnp.where(row * BLK + q * stride % BLK == column, 1.0, 0.0).astype(jnp.bfloat16)
        near = picked[q].reshape(slices * BLK, picked.shape[3])
        line = jnp.dot(pick, near, preferred_element_type=jnp.float32)
        for c in range(per_angle):
            meas[q * per_angle + c] = line[:, c * CB : (c + 1) * CB]

    def backward(k, carry):
        projected = proj[k]
        residual = (meas[index_ref[k, 0]] - projected[0:BLK]) / projected[BLK : BLK + 1]
        left = jnp.concatenate([residual, jnp.ones_like(residual)], axis=0).astype(jnp.bfloat16)
        back[k] = lax.dot_general(
            left, tiles[k], (((1,), (1,)), ((), ())), preferred_element_type=jnp.float32
        )
        return carry

    lax.fori_loop(0, tile_count, backward, 0)

    held = give.shape[1]
    for r in range(IR):

        def gather(k, total):
            same = jnp.full((held, IMG), index_ref[k, 1], jnp.int32) == r
            return total + jnp.where(same, back[k, 0:held], 0.0)

        total_of_row = lax.fori_loop(0, tile_count, gather, jnp.zeros((held, IMG), jnp.float32))
        give[r] = weight_ref[tube, 1 - tube] * total_of_row
        keep[r] = weight_ref[tube, tube] * total_of_row
    tube_copy = pltpu.make_async_remote_copy(
        src_ref=give,
        dst_ref=take,
        send_sem=tube_send,
        recv_sem=tube_recv,
        device_id={"tube": 1 - tube},
        device_id_type=MESH,
    )
    tube_copy.start()
    tube_copy.wait()
    for r in range(IR):
        part = slice(r * IMG, (r + 1) * IMG)
        both = keep[r] + take[r]
        updated_ref[:, part] = material[tube, :, part] + relax_factor * (
            both[0:BLK] / both[BLK : BLK + 1]
        )

    def last(i, carry):
        sent(groups - 1, i)
        return carry

    lax.fori_loop(0, blocks, last, 0)
    for g in range(groups):
        for v in range(views):
            if (g, v) not in early:
                arrived(g, v)

    @pl.when(slab < slabs - 1)
    def _():
        for g in range(groups):
            top_copy(g).wait_send()


def body(views, slabs, fan_views, offsets, rebin_matrix, projector, tile_index, attenuation, images):
    angles, rows, channels = fan_views.shape[2:]
    slices = images.shape[2]
    groups = angles // BLK
    blocks = rows // BLK
    share = BLK // slices
    tile_count = projector.shape[1]
    pixels = images.shape[3]
    material = images[:, 0]
    if slices < BLK:
        material = jnp.pad(material, ((0, 0), (0, BLK - slices), (0, 0)))
    held = BLK + 8
    bf16, f32 = jnp.bfloat16, jnp.float32
    dma = pltpu.SemaphoreType.DMA
    vmem = pltpu.VMEM
    smem = pl.BlockSpec(memory_space=pltpu.SMEM)
    anywhere = pl.BlockSpec(memory_space=pl.ANY)
    sinogram, updated = pl.pallas_call(
        functools.partial(kernel, (views, slabs, angles, rows, slices)),
        out_shape=(
            jax.ShapeDtypeStruct((slices, views * angles, channels), bf16),
            jax.ShapeDtypeStruct((BLK, pixels), f32),
        ),
        in_specs=[smem, smem, smem, anywhere, anywhere, anywhere, anywhere],
        out_specs=(anywhere, pl.BlockSpec(memory_space=vmem)),
        scratch_shapes=[
            vmem((angles, HZ + rows, channels), bf16),
            vmem((channels, channels), bf16),
            vmem((tile_count, IMG, CB), bf16),
            vmem((2, BLK, pixels), f32),
            vmem((groups, blocks, BLK, BLK, channels), bf16),
            vmem((IR, 2 * BLK, IMG), bf16),
            vmem((tile_count, 2 * BLK, CB), f32),
            vmem((SUB, slices, BLK, channels), bf16),
            vmem((tile_count, BLK, CB), f32),
            vmem((tile_count, 2 * BLK, IMG), f32),
            vmem((IR, held, IMG), f32),
            vmem((IR, held, IMG), f32),
            vmem((IR, held, IMG), f32),
            dma((groups,)),
            dma,
            dma,
            dma,
            dma((groups,)),
            dma((groups,)),
            dma((groups, blocks, share)),
            dma((groups, views)),
            dma((groups,)),
            dma((SUB,)),
            dma,
            dma,
        ],
        compiler_params=pltpu.CompilerParams(
            collective_id=0, has_side_effects=True, vmem_limit_bytes=48 * 1024 * 1024
        ),
        name="rebin_update",
    )(offsets[0, 0], tile_index[0], attenuation, fan_views[0, 0], rebin_matrix, projector[0], material)
    return (sinogram[None, None], updated[None, None, :slices])


def solution(mesh):
    in_specs = (
        P(("groups", "tube"), "gz", "view", None, None),
        P(("groups", "tube"), "gz", "view"),
        P(),
        P("tube", None, None, None),
        P("tube", None, None),
        P(),
        P(None, ("groups", "gz"), "view", None),
    )
    out_specs = (
        P(("groups", "tube"), "gz", "view", None, None),
        P("tube", ("groups", "gz"), "view", None),
    )
    return jax.shard_map(
        functools.partial(body, mesh.shape["view"], mesh.shape["gz"]),
        mesh=mesh,
        in_specs=in_specs,
        out_specs=out_specs,
        check_vma=False,
    )
```

time: 189 us -> 111 us (0.59)
  waiting for transfers between devices: 109 us -> 0 us
  Pallas kernels: 0 us -> 99.6 us
  local copies, waits for them, and re-layouts: 26.4 us -> 10.2 us
  matrix products: 15.1 us -> 0 us
  between operations: 14.2 us -> 0.64 us
  starting transfers between devices: 10.3 us -> 0 us
  other arithmetic: 10.2 us -> 0 us
  blocking collectives: 3.41 us -> 0 us
    pallas_call x0 -> x1, Pallas kernels: none -> 99.6 us  [body(): pl.pallas_call(functools.partial(kernel, (views, slabs, angles, rows, sli...]
    all_to_all x1 -> x0, waiting for transfers between devices: 82.7 us -> none  [body(): lax.all_to_all(outgoing, 'view', split_axis=0, concat_axis=1, tiled=True)]
    ppermute x1 -> x0, waiting for transfers between devices: 22.1 us -> none  [shifted(): return lax.ppermute(block, axis, route)]
    dot_general x9 -> x0, matrix products: 15.1 us -> none  [the longest x1 6.92 us: rebin_rows(): rebinned = jnp.dot(shaped, rebin_matrix, preferred_element_type=jnp.float32)]
    gather x1 -> x0, local copies, waits for them, and re-layouts: 12.3 us -> none  [pick_rows(): return lax.dynamic_slice_in_dim(view_rows, HZ - offset, DR, 0)]
    unnamed x17 -> x10, local copies, waits for them, and re-layouts: 3.07 us -> 9.47 us
    ppermute x1 -> x0, starting transfers between devices: 5.09 us -> none  [shifted(): return lax.ppermute(block, axis, route)]
    all_to_all x1 -> x0, local copies, waits for them, and re-layouts: 5.01 us -> none  [body(): lax.all_to_all(outgoing, 'view', split_axis=0, concat_axis=1, tiled=True)]
  transfers between devices with their start and end apart: 3 -> 0, of which waited for: 3 -> 0; matrix products, arithmetic and copies ran while one was open for 5% -> 0% of each run, Pallas kernels for 0% -> 0%
where the time goes in v1:
time: 111 us; the launch traced here: 110 us
  Pallas kernels  99.6 us (90%)
  local copies, waits for them, and re-layouts  10.2 us (9%)
    pallas_call x1, Pallas kernels, body(): pl.pallas_call(functools.partial(kernel, (views, slabs, angles, rows, sli...  99.6 us
    unnamed x10, local copies, waits for them, and re-layouts  9.47 us

profile of v1, /device:TPU:0, one launch (start us, length us, event | category | flops | bytes accessed | tf_op | source)
XLA Modules:
  0.0 110.5 jit_solution(1329721940699988428)
XLA Ops:
  0.6 0.8 copy.9.index_ref
  1.4 0.0 copy-start
  1.4 1.6 %copy-done = bf16[1024,1024]{1,0:T(8,128)(2,1)S(1)} copy-done((bf16[1024,1024]{1,0:T(8,128)(2,1)S(1)}, bf16[1024,1024]{1,0:T(8,128)(2,1)}, u32[]{:S(2)}) %copy-start) | copy-done | bytes 2097176
  3.0 0.0 copy-start.1
  3.0 1.0 copy-done.1
  4.0 0.0 copy-start.2
  4.0 0.7 copy-done.2
  4.7 0.0 copy-start.3
  4.7 0.7 copy-done.3
  5.4 99.6 %rebin_update.1 = (bf16[16,128,1024]{2,1,0:T(8,128)(2,1)}, f32[16,4096]{1,0:T(8,128)S(1)}) custom-call(s32[32]{0:T(128)S(1)} %bitcast.9, s32[16,2]{1,0:T(8,128)S(1)} %copy.9.index_ref, f32[2,2]{1,0:T(2,128)S(1)} %copy-done.2, bf16[32,64,1024]{2,1,0:T(8,128)(2,1)} %bitcast.10, bf16[1024,1024]{1,0:T(8,128)(2,1)S(1)} %copy-done, ...), custom_call_target="tpu_custom_call" | custom-call | tf_op jit(solution)/shard_map/rebin_update/pallas_call | solution.py:349
  105.0 4.8 %copy.12 = bf16[1,1,16,128,1024]{4,3,2,1,0:T(8,128)(2,1)} copy(bf16[1,1,16,128,1024]{4,3,2,1,0:T(8,128)(2,1)} %bitcast.12) | data formatting | bytes 8388608
  109.8 0.7 copy.13
Async XLA Ops:
  1.4 1.6 %copy-start = (bf16[1024,1024]{1,0:T(8,128)(2,1)S(1)}, bf16[1024,1024]{1,0:T(8,128)(2,1)}, u32[]{:S(2)}) copy-start(bf16[1024,1024]{1,0:T(8,128)(2,1)} %rebin_ref.1) | copy-start | bytes 6291460
  3.0 1.0 copy-start.1
  4.0 0.7 copy-start.2
  4.7 0.7 copy-start.3

commit v2 on v1

--- a/solution.py
+++ b/solution.py
@@ -20,15 +20,18 @@
 
 def kernel(
     sizes,
-    offsets_ref,
-    index_ref,
-    weight_ref,
+    offsets_in,
+    index_in,
+    weight_in,
     fan_ref,
     rebin_ref,
     projector_ref,
     images_ref,
     sino_ref,
     updated_ref,
+    offsets_ref,
+    index_ref,
+    weight_ref,
     ext,
     rebin,
     tiles,
@@ -54,6 +57,7 @@
     picked_sem,
     tube_send,
     tube_recv,
+    small_sem,
 ):
     views, slabs, angles, rows, slices = sizes
     groups = angles // BLK
@@ -66,22 +70,36 @@
     slab = lax.axis_index("gz")
     tube = lax.axis_index("tube")
 
-    def own_copy(g):
+    half = blocks // 2
+    low = me * slices // BLK < half
+
+    def block_of(i):
+        up = jnp.where(i < half, i + half, i - half + 1)
+        b = jnp.where(low, up, i + 1)
+        return jnp.where(i == blocks - 1, 0, b)
+
+    def own_copy(g, p):
+        chunk = lax.rem(p + jnp.where(low, half - 1, 0), blocks)
+        first = pl.multiple_of(chunk * BLK, BLK)
         return pltpu.make_async_copy(
-            fan_ref.at[pl.ds(g * BLK, BLK)],
-            ext.at[pl.ds(g * BLK, BLK), pl.ds(HZ, rows), :],
-            own_sem.at[g],
+            fan_ref.at[pl.ds(g * BLK, BLK), pl.ds(first, BLK), :],
+            ext.at[pl.ds(g * BLK, BLK), pl.ds(first + HZ, BLK), :],
+            own_sem.at[g, p],
         )
 
     rebin_copy = pltpu.make_async_copy(rebin_ref, rebin, rebin_sem)
     tiles_copy = pltpu.make_async_copy(projector_ref, tiles, tiles_sem)
     image_copy = pltpu.make_async_copy(images_ref, material, image_sem)
-    own_copy(0).start()
+    small = [
+        pltpu.make_async_copy(offsets_in, offsets_ref, small_sem.at[0]),
+        pltpu.make_async_copy(index_in, index_ref, small_sem.at[1]),
+        pltpu.make_async_copy(weight_in, weight_ref, small_sem.at[2]),
+    ]
+    for copy in small:
+        copy.start()
+    own_copy(0, 0).start()
+    own_copy(0, 1).start()
     rebin_copy.start()
-    for g in range(1, groups):
-        own_copy(g).start()
-    image_copy.start()
-    tiles_copy.start()
 
     barrier = pltpu.get_barrier_semaphore()
 
@@ -104,7 +122,6 @@
         pl.semaphore_signal(barrier, inc=1, device_id={"gz": slab + 1}, device_id_type=MESH)
 
     edges = jnp.where(slab > 0, 1, 0) + jnp.where(slab < slabs - 1, 1, 0)
-    pl.semaphore_wait(barrier, views + edges)
 
     def top_copy(g):
         return pltpu.make_async_remote_copy(
@@ -115,11 +132,6 @@
             device_id={"gz": jnp.minimum(slab + 1, slabs - 1)},
             device_id_type=MESH,
         )
-
-    @pl.when(slab < slabs - 1)
-    def _():
-        for g in range(groups):
-            top_copy(g).start()
 
     @pl.when(slab == 0)
     def _():
@@ -177,33 +189,19 @@
         def _():
             self_copy(g, 0, 0).wait()
 
-    half = blocks // 2
-    low = me * slices // BLK < half
-
-    def block_of(i):
-        up = jnp.where(i < half, i + half, i - half + 1)
-        b = jnp.where(low, up, i + 1)
-        return jnp.where(i == blocks - 1, 0, b)
-
     def work(g):
-        own_copy(g).wait()
         shape = (BLK * BLK, BLK * 2 * BLK)
         row = lax.broadcasted_iota(jnp.int32, shape, 0)
         column = lax.broadcasted_iota(jnp.int32, shape, 1)
         lane_angle = lax.broadcasted_iota(jnp.int32, (8, shape[1]), 1) >> 5
         moved = jnp.zeros((8, shape[1]), jnp.int32)
         for a in range(BLK):
-            moved = jnp.where(lane_angle == a, offsets_ref[g * BLK + a], moved)
+            moved = jnp.where(lane_angle == a, offsets_ref[0, g * BLK + a], moved)
         hit = ((row & 15) == (column >> 5)) & ((row >> 4) + HZ - (column & 31) == moved[0:1])
         chosen = jnp.where(hit, 1.0, 0.0).astype(jnp.bfloat16)
 
-        def unit(i, carry):
+        def unit(i):
             b = block_of(i)
-
-            @pl.when((i == blocks - 1) & (slab > 0))
-            def _():
-                top_copy(g).wait_recv()
-
             window = ext[pl.ds(g * BLK, BLK), pl.ds(pl.multiple_of(b * BLK, BLK), 2 * BLK), :]
             window = window.reshape(BLK * 2 * BLK, window.shape[2])
             placed = jnp.dot(chosen, window, preferred_element_type=jnp.float32)
@@ -212,13 +210,49 @@
             )
             rebinned = rebinned.astype(jnp.bfloat16)
             stage[g, b] = rebinned.reshape(BLK, BLK, rebinned.shape[1])
-            if g == 0:
-                send(g, b)
+
+        own_copy(g, 0).wait()
+        own_copy(g, 1).wait()
+        if g == 0:
+            rebin_copy.wait()
+            later()
+        unit(0)
+        if g == 0:
+            pl.semaphore_wait(barrier, views + edges)
+
+            @pl.when(slab < slabs - 1)
+            def _():
+                for h in range(groups):
+                    top_copy(h).start()
+
+        send(g, block_of(0))
+
+        def step(i, carry):
+            @pl.when(i < blocks - 1)
+            def _():
+                own_copy(g, i + 1).wait()
+
+            @pl.when((i == blocks - 1) & (slab > 0))
+            def _():
+                top_copy(g).wait_recv()
+
+            unit(i)
+            send(g, block_of(i))
             return carry
 
-        lax.fori_loop(0, blocks, unit, 0)
-
-    rebin_copy.wait()
+        lax.fori_loop(1, blocks, step, 0)
+
+    def later():
+        for p in range(2, blocks):
+            own_copy(0, p).start()
+        for g in range(1, groups):
+            for p in range(blocks):
+                own_copy(g, p).start()
+        image_copy.start()
+        tiles_copy.start()
+
+    for copy in small:
+        copy.wait()
     for g in range(groups):
         work(g)
 
@@ -233,20 +267,10 @@
     tiles_copy.wait()
 
     def forward(k, carry):
-        proj[k] = jnp.dot(comb[index_ref[k, 1]], tiles[k], preferred_element_type=jnp.float32)
+        proj[k] = jnp.dot(comb[index_ref[1, k]], tiles[k], preferred_element_type=jnp.float32)
         return carry
 
     lax.fori_loop(0, tile_count, forward, 0)
-
-    for g in range(1, groups):
-
-        def follow(i, carry):
-            b = block_of(i)
-            sent(g - 1, b)
-            send(g, b)
-            return carry
-
-        lax.fori_loop(0, blocks, follow, 0)
 
     early = []
     for q in range(SUB):
@@ -277,7 +301,7 @@
 
     def backward(k, carry):
         projected = proj[k]
-        residual = (meas[index_ref[k, 0]] - projected[0:BLK]) / projected[BLK : BLK + 1]
+        residual = (meas[index_ref[0, k]] - projected[0:BLK]) / projected[BLK : BLK + 1]
         left = jnp.concatenate([residual, jnp.ones_like(residual)], axis=0).astype(jnp.bfloat16)
         back[k] = lax.dot_general(
             left, tiles[k], (((1,), (1,)), ((), ())), preferred_element_type=jnp.float32
@@ -290,7 +314,7 @@
     for r in range(IR):
 
         def gather(k, total):
-            same = jnp.full((held, IMG), index_ref[k, 1], jnp.int32) == r
+            same = jnp.full((held, IMG), index_ref[1, k], jnp.int32) == r
             return total + jnp.where(same, back[k, 0:held], 0.0)
 
         total_of_row = lax.fori_loop(0, tile_count, gather, jnp.zeros((held, IMG), jnp.float32))
@@ -314,7 +338,8 @@
         )
 
     def last(i, carry):
-        sent(groups - 1, i)
+        for g in range(groups):
+            sent(g, i)
         return carry
 
     lax.fori_loop(0, blocks, last, 0)
@@ -344,17 +369,22 @@
     bf16, f32 = jnp.bfloat16, jnp.float32
     dma = pltpu.SemaphoreType.DMA
     vmem = pltpu.VMEM
-    smem = pl.BlockSpec(memory_space=pltpu.SMEM)
-    anywhere = pl.BlockSpec(memory_space=pl.ANY)
+    inside = slices * views * angles * channels * 2 <= 8 * 1024 * 1024
+    landing = vmem if inside else jax.ShapeDtypeStruct
+    where = pl.BlockSpec(memory_space=vmem if inside else pl.ANY)
+    hbm = pl.BlockSpec(memory_space=pltpu.HBM)
     sinogram, updated = pl.pallas_call(
         functools.partial(kernel, (views, slabs, angles, rows, slices)),
         out_shape=(
-            jax.ShapeDtypeStruct((slices, views * angles, channels), bf16),
-            jax.ShapeDtypeStruct((BLK, pixels), f32),
+            landing((slices, views * angles, channels), bf16),
+            vmem((BLK, pixels), f32),
         ),
-        in_specs=[smem, smem, smem, anywhere, anywhere, anywhere, anywhere],
-        out_specs=(anywhere, pl.BlockSpec(memory_space=vmem)),
+        in_specs=[hbm] * 7,
+        out_specs=(where, pl.BlockSpec(memory_space=vmem)),
         scratch_shapes=[
+            pltpu.SMEM((1, angles), jnp.int32),
+            pltpu.SMEM((2, tile_count), jnp.int32),
+            pltpu.SMEM((2, 2), f32),
             vmem((angles, HZ + rows, channels), bf16),
             vmem((channels, channels), bf16),
             vmem((tile_count, IMG, CB), bf16),
@@ -368,7 +398,7 @@
             vmem((IR, held, IMG), f32),
             vmem((IR, held, IMG), f32),
             vmem((IR, held, IMG), f32),
-            dma((groups,)),
+            dma((groups, blocks)),
             dma,
             dma,
             dma,
@@ -380,12 +410,13 @@
             dma((SUB,)),
             dma,
             dma,
+            dma((3,)),
         ],
         compiler_params=pltpu.CompilerParams(
-            collective_id=0, has_side_effects=True, vmem_limit_bytes=48 * 1024 * 1024
+            collective_id=0, has_side_effects=True, vmem_limit_bytes=119 * 512 * 1024
         ),
         name="rebin_update",
-    )(offsets[0, 0], tile_index[0], attenuation, fan_views[0, 0], rebin_matrix, projector[0], material)
+    )(offsets[0], tile_index[0].T, attenuation, fan_views[0, 0], rebin_matrix, projector[0], material)
     return (sinogram[None, None], updated[None, None, :slices])
 
 

time: 111 us -> 101 us (0.910)
  local copies, waits for them, and re-layouts: 10.2 us -> 2.72 us
  Pallas kernels: 99.6 us -> 97.9 us
    unnamed x10 -> x2, local copies, waits for them, and re-layouts: 9.47 us -> 2.72 us
    pallas_call x1, Pallas kernels: 99.6 us -> 97.9 us  [body(): pl.pallas_call(functools.partial(kernel, (views, slabs, angles, rows, sli...]
where the time goes in v2:
time: 101 us
  Pallas kernels  97.9 us (97%)
  local copies, waits for them, and re-layouts  2.72 us (3%)
    pallas_call x1, Pallas kernels, body(): pl.pallas_call(functools.partial(kernel, (views, slabs, angles, rows, sli...  97.9 us
    unnamed x2, local copies, waits for them, and re-layouts  2.72 us

profile of v2, /device:TPU:0, one launch (start us, length us, event | category | flops | bytes accessed | tf_op | source)
XLA Modules:
  0.0 101.2 jit_solution(18178955718005494198)
XLA Ops:
  0.6 97.9 %rebin_update.1 = (bf16[16,128,1024]{2,1,0:T(8,128)(2,1)S(1)}, f32[16,4096]{1,0:T(8,128)S(1)}) custom-call(s32[1,32]{1,0:T(1,128)} %bitcast.15, s32[2,16]{1,0:T(2,128)} %bitcast.14, f32[2,2]{1,0:T(2,128)} %weight_in.1, bf16[32,64,1024]{2,1,0:T(8,128)(2,1)} %bitcast.11, bf16[1024,1024]{1,0:T(8,128)(2,1)} %rebin_ref.1, bf16[16,512,256]{2,1,0:T(8,128)(2,1)} %bitcast.12, ...), custom_call_target="tpu_custom_call" | custom-call | tf_op jit(solution)/shard_map/rebin_update/pallas_call | solution.py:376
  98.5 2.0 %copy.11 = bf16[1,1,16,128,1024]{4,3,2,1,0:T(8,128)(2,1)} copy(bf16[1,1,16,128,1024]{4,3,2,1,0:T(8,128)(2,1)S(1)} %bitcast.9) | data formatting | bytes 8388608
  100.5 0.7 copy.12
